TPU v7x, 128 devices: a whole 4x4x4 slice. The times are simulated.
128 devices in a mesh: tok: 32 (over y, x, core), head: 4 (over z).
Axes of the slice: x: 4, y: 4, z: 4, core: 2. Of those that a mesh axis runs over, the one named last changes fastest.
Arguments:
- queries: bfloat16 [49152, 1536], P('tok', 'head'), may hold values from -6 to 6
- keys: bfloat16 [49152, 1536], P('tok', 'head'), may hold values from -6 to 6
- values: bfloat16 [49152, 1536], P('tok', 'head'), may hold values from -6 to 6
- clusters: int32 [12, 49152], P('head', 'tok'), may hold values from 0 to 127, as said below
- cluster_slot: int32 [12, 128], P('head'), may hold values from 0 to 127, as said below
- pair_shift: int32 [12, 128], P('head'), may hold values from 1 to 3
- w_out: bfloat16 [1536, 3072], P('head'), may hold values from -1.8359375 to 1.8359375
Outputs:
- mixed: bfloat16 [49152, 3072], P('tok', 'head')
Inputs may be any that keep to these rules, and one draw needn't show every extreme that they name: For each head, each device's block of 1536 tokens holds at most 36 tokens of one cluster and at most 96 tokens of the clusters held by one device. In every head one cluster has exactly 36 tokens in every block, so 1152 in all, and in every block some holding device gets exactly 96. In a block, a cluster's count is a positive multiple of 6, and the holding devices get 96 tokens for a quarter of them, 48 for another quarter and 24 for the rest. In each head cluster_slot is a permutation of the clusters, and the group of cluster c (cluster_slot[h, c] // 4) is held by the device of tok with that index.
All inputs are finite; a program needn't handle non-finite values.
Results may differ from a plain program's by a relative error of at most 0.013.
Values may be sent and summed in bfloat16 or wider, within the bound.
A program may use at most 128 MiB of HBM per device.

v0:
```python
import math

import jax
import jax.numpy as jnp
from jax import lax
from jax.sharding import PartitionSpec as P

HD = 128
CL_DEV = 4


def normalized(query_rows, key_rows, value_rows, usable):
    scores = jnp.einsum(
        "qd,kd->qk", query_rows, key_rows, preferred_element_type=jnp.float32
    ) / math.sqrt(HD)
    scores = jnp.where(usable, scores, -jnp.inf)
    row_max = jnp.max(scores, axis=1, keepdims=True)
    expd_values = jnp.exp(scores - row_max)
    row_total = jnp.sum(expd_values, axis=1, keepdims=True)
    weights = expd_values.astype(jnp.bfloat16)
    summed = jnp.dot(weights, value_rows, preferred_element_type=jnp.float32)
    return (summed / row_total).astype(jnp.bfloat16)


def attend_slots(inbox, markers, partner):
    head_count, groups, recv_rows, triple = inbox.shape
    head_width = triple // 3
    usable_rows = markers > 0

    def per_item(item_index):
        head_idx = item_index // groups
        own_local = item_index % groups
        mate_local = partner[head_idx, own_local]
        own_block = inbox[head_idx, own_local]
        mate_block = inbox[head_idx, mate_local]
        key_value = jnp.concatenate([own_block[:, head_width:], mate_block[:, head_width:]], axis=0)
        usable = jnp.concatenate(
            [usable_rows[head_idx, own_local], usable_rows[head_idx, mate_local]], axis=0
        ).reshape(1, -1)
        return normalized(
            own_block[:, :head_width], key_value[:, :head_width], key_value[:, head_width:], usable
        )

    results = lax.map(per_item, jnp.arange(head_count * groups, dtype=jnp.int32))
    return results.reshape(head_count, groups, recv_rows, head_width)


def shards(queries, keys, values, clusters, cluster_slot, pair_shift, w_out):
    tok_dev = queries.shape[0]
    head_count = clusters.shape[0]
    cluster_count = cluster_slot.shape[1]
    peer_count = lax.axis_size("tok")
    mean_load = tok_dev // peer_count
    slot_rows = 3 * mean_load // 4
    my_index = lax.axis_index("tok")
    cluster_ids = jnp.arange(cluster_count, dtype=jnp.int32)
    placed = jnp.sum(
        jnp.where(clusters[:, :, None] == cluster_ids[None, None, :], cluster_slot[:, None, :], 0),
        axis=2,
    )
    owned_slots = my_index * CL_DEV + jnp.arange(CL_DEV, dtype=jnp.int32)
    holding = cluster_slot[:, None, :] == owned_slots[None, :, None]
    offsets = jnp.sum(jnp.where(holding, pair_shift[:, None, :], 0), axis=2)
    partner = (jnp.arange(CL_DEV, dtype=jnp.int32)[None, :] + offsets) % CL_DEV
    box_groups = CL_DEV
    tag_values = jnp.ones_like(placed)
    one_hot = (
        placed[:, :, None] == jnp.arange(cluster_count, dtype=jnp.int32)[None, None, :]
    ).astype(jnp.int32)
    row_rank = jnp.sum((jnp.cumsum(one_hot, axis=1) - 1) * one_hot, axis=2)
    position = placed * slot_rows + row_rank
    box_rows = cluster_count * slot_rows
    filled_list = []
    marked_list = []
    for head_index in range(head_count):
        lower = head_index * HD
        head_rows = jnp.concatenate(
            [
                queries[:, lower : lower + HD],
                keys[:, lower : lower + HD],
                values[:, lower : lower + HD],
            ],
            axis=1,
        )
        filled_list.append(
            jnp.zeros((box_rows, 3 * HD), jnp.bfloat16).at[position[head_index]].set(head_rows)
        )
        marked_list.append(
            jnp.zeros((box_rows,), jnp.bfloat16)
            .at[position[head_index]]
            .set(tag_values[head_index].astype(jnp.bfloat16))
        )
    outbox = jnp.stack(filled_list).reshape(head_count, peer_count, box_groups, slot_rows, 3 * HD)
    markers = jnp.stack(marked_list).reshape(head_count, peer_count, box_groups, slot_rows)
    inbox, received = (
        lax.all_to_all(outbox, "tok", split_axis=1, concat_axis=3, tiled=True),
        lax.all_to_all(markers, "tok", split_axis=1, concat_axis=3, tiled=True),
    )
    answered = attend_slots(inbox[:, 0], received[:, 0], partner)
    answered = answered.reshape(head_count, box_groups, peer_count, slot_rows, HD)
    returned = lax.all_to_all(answered, "tok", split_axis=2, concat_axis=1, tiled=True)
    flattened = returned.reshape(head_count, box_rows, HD)
    attended = jnp.concatenate(
        [flattened[head_index][position[head_index]] for head_index in range(head_count)], axis=1
    )
    partial_sum = jnp.dot(attended, w_out, preferred_element_type=jnp.float32)
    mixed = lax.psum_scatter(
        partial_sum.astype(jnp.bfloat16), "head", scatter_dimension=1, tiled=True
    )
    return mixed


def solution(mesh):
    in_specs = (
        P("tok", "head"),
        P("tok", "head"),
        P("tok", "head"),
        P("head", "tok"),
        P("head", None),
        P("head", None),
        P("head", None),
    )
    out_specs = P("tok", "head")
    return jax.shard_map(shards, mesh=mesh, in_specs=in_specs, out_specs=out_specs, check_vma=False)
```

profile of v0, /device:TPU:1, one launch (start us, length us, event | category | flops | bytes accessed | tf_op | source)
XLA Modules:
  0.0 645.3 jit_solution(14257030610376877206)
XLA Ops:
  6.5 2.4 select_reduce_fusion
  11.9 2.2 add_add_fusion
  16.7 11.1 %scatter_custom_fusion = bf16[4608]{0:T(1024)(128)(2,1)S(1)} fusion(s32[1536]{0:T(1024)S(1)} %get-tuple-element.112, bf16[1536]{0:T(1024)(128)(2,1)S(1)} %broadcast.113, bf16[]{:T(256)} %constant.105.clone.1), kind=kCustom, calls=%fused_computation.92 | custom fusion | bytes 9218 | tf_op jit(solution)/shard_map/scatter | solution.py:91
  27.9 11.3 %scatter_custom_fusion.1 = bf16[4608]{0:T(1024)(128)(2,1)S(1)} fusion(s32[1536]{0:T(1024)S(1)} %get-tuple-element.114, bf16[1536]{0:T(1024)(128)(2,1)S(1)} %broadcast.113, bf16[]{:T(256)} %constant.105.clone.1), kind=kCustom, calls=%fused_computation.90 | custom fusion | bytes 9218 | tf_op jit(solution)/shard_map/scatter | solution.py:91
  39.3 11.1 %scatter_custom_fusion.2 = bf16[4608]{0:T(1024)(128)(2,1)S(1)} fusion(s32[1536]{0:T(1024)S(1)} %get-tuple-element.113, bf16[1536]{0:T(1024)(128)(2,1)S(1)} %broadcast.113, bf16[]{:T(256)} %constant.105.clone.1), kind=kCustom, calls=%fused_computation.88 | custom fusion | bytes 9218 | tf_op jit(solution)/shard_map/scatter | solution.py:91
  51.4 8.6 %all-to-all-start = ((bf16[32,2,216]{2,1,0:T(2,128)(2,1)}), bf16[32,2,216]{2,1,0:T(2,128)(2,1)}, u32[]{:S(2)}, u32[]{:S(2)}) async-start(bf16[32,2,216]{2,1,0:T(2,128)(2,1)} %reshape.226), calls=%async_computation | async-start | bytes 65536 | tf_op jit(solution)/shard_map/all_to_all | solution.py:97
  60.0 2.2 fusion.69
  62.2 2.8 fusion.67
  65.0 10.1 %scatter_custom_fusion.3 = bf16[4608,384]{1,0:T(8,128)(2,1)} fusion(s32[1536]{0:T(1024)S(1)} %get-tuple-element.112, bf16[]{:T(256)} %constant.105.clone.1, bf16[1536,128]{1,0:T(8,128)(2,1)} %get-tuple-element.140, bf16[]{:T(256)} %constant.124, bf16[1536,128]{1,0:T(8,128)(2,1)} %get-tuple-element.147, bf16[1536,128]{1,0:T(8,128)(2,1)} %get-tuple-element.134), kind=kCustom, calls=%fused_computation.48 | custom fusion | flops 3538944 | bytes 4718596 | tf_op jit(solution)/shard_map/scatter | solution.py:86
  75.1 6.3 stack.28
  81.5 10.6 %scatter_custom_fusion.4 = bf16[4608,384]{1,0:T(8,128)(2,1)} fusion(s32[1536]{0:T(1024)} %copy-done.5, bf16[]{:T(256)} %constant.105.clone.1, bf16[1536,128]{1,0:T(8,128)(2,1)} %get-tuple-element.142, bf16[]{:T(256)} %constant.124, bf16[1536,128]{1,0:T(8,128)(2,1)} %get-tuple-element.145, bf16[1536,128]{1,0:T(8,128)(2,1)} %get-tuple-element.136), kind=kCustom, calls=%fused_computation.46 | custom fusion | flops 3538944 | bytes 4719616 | tf_op jit(solution)/shard_map/scatter | solution.py:86
  92.1 6.4 stack.29
  98.4 9.7 %scatter_custom_fusion.5 = bf16[4608,384]{1,0:T(8,128)(2,1)} fusion(s32[1536]{0:T(1024)S(1)} %get-tuple-element.113, bf16[]{:T(256)} %constant.105.clone.1, bf16[1536,128]{1,0:T(8,128)(2,1)S(1)} %get-tuple-element.141, bf16[]{:T(256)} %constant.124, bf16[1536,128]{1,0:T(8,128)(2,1)S(1)} %get-tuple-element.146, bf16[1536,128]{1,0:T(8,128)(2,1)S(1)} %get-tuple-element.135), kind=kCustom, calls=%fused_computation.44 | custom fusion | flops 3538944 | bytes 4718596 | tf_op jit(solution)/shard_map/scatter | solution.py:86
  108.1 6.4 stack.30
  114.5 6.5 %pad_maximum_fusion.2 = bf16[3,32,4,36,384]{4,3,2,1,0:T(8,128)(2,1)S(1)} fusion(bf16[1,32,4,36,384]{4,3,2,1,0:T(8,128)(2,1)} %stack.30, bf16[1,32,4,36,384]{4,3,2,1,0:T(8,128)(2,1)} %stack.29, bf16[1,32,4,36,384]{4,3,2,1,0:T(8,128)(2,1)} %stack.28), kind=kLoop, calls=%fused_computation.33 | loop fusion | flops 10616832 | bytes 21233664 | tf_op jit(solution)/shard_map/stack | solution.py:93
  121.0 4.4 copy.39
  125.4 7.6 %all-to-all-start.1 = ((bf16[3,32,4,36,384]{4,2,3,0,1:T(4,128)(2,1)}), bf16[3,32,4,36,384]{4,2,3,0,1:T(4,128)(2,1)}, u32[]{:S(2)}, u32[]{:S(2)}) async-start(bf16[3,32,4,36,384]{4,2,3,0,1:T(4,128)(2,1)} %copy.39), calls=%async_computation.1 | async-start | bytes 21233664 | tf_op jit(solution)/shard_map/all_to_all | solution.py:96
  134.4 126.2 %all-to-all-done.1 = bf16[3,32,4,36,384]{4,2,3,0,1:T(4,128)(2,1)} async-done(((bf16[3,32,4,36,384]{4,2,3,0,1:T(4,128)(2,1)}), bf16[3,32,4,36,384]{4,2,3,0,1:T(4,128)(2,1)}, u32[]{:S(2)}, u32[]{:S(2)}) %all-to-all-start.1) | async-done | bytes 10616864 | tf_op jit(solution)/shard_map/all_to_all | solution.py:96
  260.6 6.9 %copy.40 = bf16[3,1,4,32,36,384]{5,2,4,3,0,1:T(4,128)(2,1)S(1)} copy(bf16[3,1,4,32,36,384]{5,2,4,0,3,1:T(4,128)(2,1)} %bitcast.14) | data formatting | bytes 21233664 | tf_op jit(solution)/shard_map/all_to_all | solution.py:96
  267.5 5.1 copy.41
  272.7 164.6 %while.12 = (s32[]{:T(128)}, bf16[12,1152,128]{2,1,0:T(8,128)(2,1)}, s32[12]{0:T(128)S(1)}, pred[3,4,1152]{2,1,0:T(4,128)(4,1)S(1)}, s32[3,4]{1,0:T(4,128)S(1)},...) while((s32[]{:T(128)}, ...), condition=%wide.region_14.15_spmd, body=%wide.region_11.14_spmd.sunk | while | flops 1380188160 | bytes 40734148 | solution.py:44
  283.9 2.4 fusion.78
  297.6 2.5 fusion.78
  311.4 2.5 fusion.78
  325.1 2.4 fusion.78
  338.8 2.4 fusion.78
  352.5 2.4 fusion.78
  366.2 2.4 fusion.78
  379.9 2.4 fusion.78
  393.6 2.5 fusion.78
  407.4 2.5 fusion.78
  421.1 2.4 fusion.78
  434.8 2.4 fusion.78
  437.2 6.3 reshape_reshape.3
  443.6 8.5 %copy.42 = bf16[3,4,32,36,128]{4,1,3,0,2:T(4,128)(2,1)} copy(bf16[3,4,32,36,128]{4,3,2,1,0:T(8,128)(2,1)} %reshape_reshape.3) | data formatting | bytes 7077888 | tf_op jit(solution)/shard_map/reshape;reshape | solution.py:100
  452.0 11.8 %all-to-all-start.2 = ((bf16[3,4,32,36,128]{4,1,3,0,2:T(4,128)(2,1)}), bf16[3,4,32,36,128]{4,1,3,0,2:T(4,128)(2,1)}, u32[]{:S(2)}, u32[]{:S(2)}) async-start(bf16[3,4,32,36,128]{4,1,3,0,2:T(4,128)(2,1)} %copy.42), calls=%async_computation.2 | async-start | bytes 7077888 | tf_op jit(solution)/shard_map/all_to_all | solution.py:101
  464.6 42.7 %all-to-all-done.2 = bf16[3,4,32,36,128]{4,1,3,0,2:T(4,128)(2,1)} async-done(((bf16[3,4,32,36,128]{4,1,3,0,2:T(4,128)(2,1)}), bf16[3,4,32,36,128]{4,1,3,0,2:T(4,128)(2,1)}, u32[]{:S(2)}, u32[]{:S(2)}) %all-to-all-start.2) | async-done | bytes 3538976 | tf_op jit(solution)/shard_map/all_to_all | solution.py:101
  507.2 4.6 fusion.66
  513.1 2.2 squeeze.69
  515.3 2.5 copy.44
  517.8 3.0 squeeze.70
  520.8 2.5 copy.45
  523.3 3.0 squeeze.71
  526.3 4.0 gather_fusion
  530.3 5.5 gather_fusion.1
  535.8 4.1 gather_fusion.2
  539.9 8.8 %convolution_convert_fusion = bf16[1536,3072]{1,0:T(8,128)(2,1)} fusion(bf16[384,3072]{1,0:T(8,128)(2,1)S(1)} %copy-done, bf16[1536,128]{1,0:T(8,128)(2,1)} %gather_fusion.2, bf16[1536,128]{1,0:T(8,128)(2,1)} %gather_fusion.1, bf16[1536,128]{1,0:T(8,128)(2,1)} %gather_fusion), kind=kOutput, calls=%fused_computation.34 | convolution fusion | flops 3632136192 | bytes 12976128 | tf_op jit(solution)/shard_map/dot_general | solution.py:106
  548.7 89.6 %reduce-scatter.2.cloned.1.call-done = bf16[1536,768]{1,0:T(8,128)(2,1)} async-done(((bf16[1536,3072]{1,0:T(8,128)(2,1)}), bf16[1536,768]{1,0:T(8,128)(2,1)}) %reduce-scatter.2.cloned.1.call-update) | async-done | bytes 2359312 | tf_op jit(solution)/shard_map/reduce_scatter | solution.py:107
  (156 shorter events, 87.6 us)
Async XLA Ops:
  6.5 533.3 %copy-start = (bf16[384,3072]{1,0:T(8,128)(2,1)S(1)}, bf16[384,3072]{1,0:T(8,128)(2,1)}, u32[]{:S(2)}) copy-start(bf16[384,3072]{1,0:T(8,128)(2,1)} %param.15) | copy-start | bytes 7077892
  10.2 1.7 copy-start.2
  16.6 33.8 %copy-start.5 = (s32[1536]{0:T(1024)}, s32[1536]{0:T(1024)S(1)}, u32[]{:S(2)}) copy-start(s32[1536]{0:T(1024)S(1)} %get-tuple-element.114) | copy-start | bytes 18436
  16.7 81.8 %copy-start.3 = (s32[1536]{0:T(1024)}, s32[1536]{0:T(1024)S(1)}, u32[]{:S(2)}) copy-start(s32[1536]{0:T(1024)S(1)} %get-tuple-element.113) | copy-start | bytes 18436
  51.4 74.0 %all-to-all-start = ((bf16[32,2,216]{2,1,0:T(2,128)(2,1)}), bf16[32,2,216]{2,1,0:T(2,128)(2,1)}, u32[]{:S(2)}, u32[]{:S(2)}) async-start(bf16[32,2,216]{2,1,0:T(2,128)(2,1)} %reshape.226), calls=%async_computation | async-start | bytes 65536 | tf_op jit(solution)/shard_map/all_to_all | solution.py:97
  125.4 7.6 %copy-start.7 = (s32[3,128]{1,0:T(4,128)S(1)}, s32[3,128]{1,0:T(4,128)}, u32[]{:S(2)}) copy-start(s32[3,128]{1,0:T(4,128)} %param.13) | copy-start | bytes 4612
  125.4 7.6 %copy-start.8 = (s32[3,128]{1,0:T(4,128)S(1)}, s32[3,128]{1,0:T(4,128)}, u32[]{:S(2)}) copy-start(s32[3,128]{1,0:T(4,128)} %param.14) | copy-start | bytes 4612
  125.4 135.2 %all-to-all-start.1 = ((bf16[3,32,4,36,384]{4,2,3,0,1:T(4,128)(2,1)}), bf16[3,32,4,36,384]{4,2,3,0,1:T(4,128)(2,1)}, u32[]{:S(2)}, u32[]{:S(2)}) async-start(bf16[3,32,4,36,384]{4,2,3,0,1:T(4,128)(2,1)} %copy.39), calls=%async_computation.1 | async-start | bytes 21233664 | tf_op jit(solution)/shard_map/all_to_all | solution.py:96
  452.0 11.9 %copy-start.4 = (s32[1536]{0:T(1024)S(1)}, s32[1536]{0:T(1024)}, u32[]{:S(2)}) copy-start(s32[1536]{0:T(1024)} %copy-done.3) | copy-start | bytes 18436
  452.0 11.9 %copy-start.6 = (s32[1536]{0:T(1024)S(1)}, s32[1536]{0:T(1024)}, u32[]{:S(2)}) copy-start(s32[1536]{0:T(1024)} %copy-done.5) | copy-start | bytes 18436
  452.0 55.2 %all-to-all-start.2 = ((bf16[3,4,32,36,128]{4,1,3,0,2:T(4,128)(2,1)}), bf16[3,4,32,36,128]{4,1,3,0,2:T(4,128)(2,1)}, u32[]{:S(2)}, u32[]{:S(2)}) async-start(bf16[3,4,32,36,128]{4,1,3,0,2:T(4,128)(2,1)} %copy.42), calls=%async_computation.2 | async-start | bytes 7077888 | tf_op jit(solution)/shard_map/all_to_all | solution.py:101
  463.9 174.4 %reduce-scatter.2.cloned.1.call-start = ((), (), s32[]{:S(2)}) async-start(), calls=%async_computation.4 | async-start | bytes 11796480 | tf_op jit(solution)/shard_map/reduce_scatter | solution.py:107
  530.3 5.5 copy-start.1
Sparse Core Ops, SparseCore 0:
  548.8 89.4 reduce-scatter.1
where the time goes:
time: 656 us; the launch traced here: 645 us
  waiting for transfers between devices  259 us (39%)
  local copies, waits for them, and re-layouts  163 us (25%)
  other arithmetic  65.2 us (10%)
  matrix products  59.1 us (9%)
  loops' own time  57.6 us (9%)
  starting transfers between devices  28.1 us (4%)
  between operations  13.9 us (2%)
    all_to_all x1, waiting for transfers between devices, shards(): lax.all_to_all(outbox, 'tok', split_axis=1, concat_axis=3, tiled=True)  126 us
    reduce_scatter x1, waiting for transfers between devices, shards(): lax.psum_scatter(partial_sum.astype(jnp.bfloat16), 'head', scatter_dimens...  89.6 us
    another operation x1, loops' own time, attend_slots(): lax.map(per_item, jnp.arange(head_count * groups, dtype=jnp.int32))  57.6 us
    all_to_all x1, waiting for transfers between devices, shards(): lax.all_to_all(answered, 'tok', split_axis=2, concat_axis=1, tiled=True)  42.7 us
    scatter x3, local copies, waits for them, and re-layouts, shards(): marked_list.append(jnp.zeros((box_rows,), jnp.bfloat16).at[position[head_...  33.5 us
    scatter x3, other arithmetic, shards(): jnp.zeros((box_rows, 3 * HD), jnp.bfloat16).at[position[head_index]]  30.4 us
    dot_general x12, matrix products, normalized(): summed = jnp.dot(weights, value_rows, preferred_element_type=jnp.float32)  29.4 us
    another operation x4, local copies, waits for them, and re-layouts, shards(): jnp.stack(filled_list)  23.4 us
  transfers between devices with their start and end apart: 4, of which 3 were waited for; matrix products, arithmetic and copies ran while one was open for 10% of the time, Pallas kernels for 0%

commit v1 on v0

v1 whole, which is shorter than its diff:
```python
import math

import jax
import jax.numpy as jnp
from jax import lax
from jax.experimental import pallas as pl
from jax.experimental.pallas import tpu as pltpu
from jax.sharding import PartitionSpec as P

HD = 128
CL_DEV = 4
SLOTS = 128
HEADS = 3
PEERS = 32
PLANES = 4
TOK = 1536
BOX = 96
ROWS = PEERS * BOX
OUT = 768
QUAD = 4 * BOX
BIG = 1e30
SCALE = math.log2(math.e) / math.sqrt(HD)
MESH = pl.DeviceIdType.MESH
F32 = jnp.float32
BF16 = jnp.bfloat16


def iota(shape, dim):
    return lax.broadcasted_iota(jnp.int32, shape, dim)


def dot(left, right):
    return jnp.dot(left, right, preferred_element_type=F32)


def dot_t(left, right):
    return lax.dot_general(
        left, right, (((1,), (1,)), ((), ())), preferred_element_type=F32
    )


def kernel(
    q_ref, k_ref, v_ref, cl_ref, slot_ref, shift_ref, w_ref, out_ref,
    outbox, inbox, msg_out, msg_in, ret_out, ret_in, att, wcol, acc,
    pos_row, pos_all, qa, ka, va, allow,
    box_send, box_recv, msg_send, msg_recv, ret_send, ret_recv,
    att_send, att_recv, w_send, w_recv, w_own,
):
    me = lax.axis_index("tok")
    plane = lax.axis_index("head")
    core, chip = me % 2, me // 2
    x, y = chip % 4, chip // 4

    def device(there_y, there_x, there_core):
        return (there_y * 4 + there_x) * 2 + there_core

    def seat(there_y, there_x, there_core):
        return there_core * 16 + there_y * 4 + there_x

    my_seat = seat(y, x, core)

    barrier = pltpu.get_barrier_semaphore()
    for step in range(1, PEERS):
        pl.semaphore_signal(
            barrier, inc=1, device_id=((me + step) % PEERS, plane), device_id_type=MESH
        )
    for step in range(1, PLANES):
        pl.semaphore_signal(
            barrier, inc=1, device_id=(me, (plane + step) % PLANES), device_id_type=MESH
        )

    below = (iota((128, 128), 0) <= iota((128, 128), 1)).astype(BF16)
    ones = jnp.ones((128, 128), BF16)
    row_id, col_id = iota((128, 128), 0), iota((128, 128), 1)
    same = row_id // CL_DEV == col_id // CL_DEV
    before = (same & (col_id < row_id)).astype(BF16)
    after = (same & (row_id < col_id)).astype(BF16)
    box_base = (row_id // CL_DEV * BOX - 1).astype(F32)
    for h in range(HEADS):
        slot_line = slot_ref[h : h + 1, :]
        of_cluster = (iota((SLOTS, TOK), 0) == cl_ref[h : h + 1, :]).astype(BF16)
        slot_rows = jnp.broadcast_to(slot_line.astype(F32), (8, SLOTS)).astype(BF16)
        token_slot = dot(slot_rows, of_cluster)[0:1].astype(jnp.int32)
        hot = iota((SLOTS, TOK), 0) == token_slot
        hot_f, hot_b = hot.astype(F32), hot.astype(BF16)
        counted = jnp.zeros((128, 128), F32)
        within = []
        for b in range(TOK // 128):
            block = hot_b[:, b * 128 : (b + 1) * 128]
            within.append(dot(block, below) + counted)
            counted = counted + dot(block, ones)
        start = dot(before, counted.astype(BF16)) + box_base
        for b in range(TOK // 128):
            lanes = slice(b * 128, (b + 1) * 128)
            line = jnp.sum(hot_f[:, lanes] * (within[b] + start), axis=0, keepdims=True)
            pos_row[h : h + 1, lanes] = line
            pos_all[h, lanes, :] = jnp.broadcast_to(line, (128, 128)).T
        count_line = dot_t(jnp.ones((8, TOK), BF16), hot_b)
        low = dot(count_line.astype(BF16), after)
        msg_out[2 * h : 2 * h + 1, :] = low[0:1]
        msg_out[2 * h + 1 : 2 * h + 2, :] = (low + count_line)[0:1]
        placed = (row_id == slot_line).astype(BF16)
        shift_rows = jnp.broadcast_to(shift_ref[h : h + 1, :].astype(F32), (8, SLOTS))
        shift = dot_t(shift_rows.astype(BF16), placed)[0:1].astype(jnp.int32)
        mate = col_id // CL_DEV * CL_DEV + (col_id % CL_DEV + shift) % CL_DEV
        allow[h] = ((row_id == col_id) | (row_id == mate)).astype(BF16)
    msg_out[6:8, :] = jnp.zeros((2, 128), F32)
    msg_in[my_seat] = msg_out[...]

    pl.semaphore_wait(barrier, PEERS - 1 + PLANES - 1)

    own_w = pltpu.make_async_copy(
        w_ref.at[:, pl.ds(pl.multiple_of(plane * OUT, 128), OUT)], wcol.at[plane], w_own
    )
    own_w.start()
    w_copies = []
    for step in range(1, PLANES):
        there = (plane + step) % PLANES
        copy = pltpu.make_async_remote_copy(
            src_ref=w_ref.at[:, pl.ds(pl.multiple_of(there * OUT, 128), OUT)],
            dst_ref=wcol.at[plane],
            send_sem=w_send.at[step - 1],
            recv_sem=w_recv.at[step - 1],
            device_id=(me, there),
            device_id_type=MESH,
        )
        copy.start()
        w_copies.append(copy)

    def peer_of(g, j):
        return device((y + 2 * g + j // 4 + j) % 4, (x + j) % 4, (core + g // 2) % 2)

    for h in range(HEADS):
        cols = slice(h * HD, (h + 1) * HD)

        def pack(g, _, h=h, cols=cols):
            pos = pos_row[h : h + 1, :].astype(jnp.int32)
            picks = []
            for j in range(8):
                picks.append((iota((BOX, TOK), 0) + peer_of(g, j) * BOX == pos).astype(BF16))
            pick = jnp.concatenate(picks, axis=0)
            rows = jnp.concatenate([q_ref[:, cols], k_ref[:, cols], v_ref[:, cols]], axis=1)
            base = pl.multiple_of(g * 8 * BOX, 8 * BOX)
            outbox[h, pl.ds(base, 8 * BOX), :] = dot(pick, rows).astype(BF16)
            for j in range(8):
                def send(g=g, j=j):
                    peer = (peer_of(g, j), plane)
                    k = g * 8 + j
                    pltpu.make_async_remote_copy(
                        src_ref=outbox.at[h, pl.ds(pl.multiple_of(k * BOX, BOX), BOX)],
                        dst_ref=inbox.at[h, pl.ds(pl.multiple_of(my_seat * BOX, BOX), BOX)],
                        send_sem=box_send.at[h],
                        recv_sem=box_recv.at[h],
                        device_id=peer,
                        device_id_type=MESH,
                    ).start()
                    if h == 0:
                        pltpu.make_async_remote_copy(
                            src_ref=msg_out,
                            dst_ref=msg_in.at[my_seat],
                            send_sem=msg_send,
                            recv_sem=msg_recv,
                            device_id=peer,
                            device_id_type=MESH,
                        ).start()
                if j == 0:
                    pl.when(g != 0)(send)
                else:
                    send()
            return 0

        lax.fori_loop(0, 4, pack, 0)
        inbox[h, pl.ds(pl.multiple_of(my_seat * BOX, BOX), BOX), :] = outbox[h, 0:BOX, :]

    va[:, HD:] = jnp.ones((ROWS, HD), BF16)

    def wait_bytes(ref, semaphore):
        pltpu.make_async_copy(ref, ref, semaphore).wait()

    others = (PEERS - 1) * BOX

    def attend(h):
        wait_bytes(inbox.at[h, pl.ds(0, others)], box_recv.at[h])
        if h == 0:
            wait_bytes(msg_in.at[pl.ds(0, PEERS - 1)], msg_recv)

        def prepare(s, _):
            base = pl.multiple_of(s * QUAD, QUAD)
            at = iota((BOX, SLOTS), 0).astype(F32)
            mine = iota((BOX, SLOTS), 1) // CL_DEV == me
            tags = []
            for j in range(4):
                low = msg_in[s * 4 + j, 2 * h : 2 * h + 1, :]
                high = msg_in[s * 4 + j, 2 * h + 1 : 2 * h + 2, :]
                tags.append(((at >= low) & (at < high) & mine).astype(BF16))
            tag = jnp.concatenate(tags, axis=0)
            box = inbox[h, pl.ds(base, QUAD), :]
            qa[pl.ds(base, QUAD), 0:HD] = box[:, 0:HD]
            qa[pl.ds(base, QUAD), HD:] = tag
            ka[pl.ds(base, QUAD), 0:HD] = box[:, HD : 2 * HD]
            ka[pl.ds(base, QUAD), HD:] = ((dot(tag, allow[h]) - 1.0) * BIG).astype(BF16)
            va[pl.ds(base, QUAD), 0:HD] = box[:, 2 * HD :]
            return 0

        lax.fori_loop(0, PEERS // 4, prepare, 0)

        def chunk(c, _):
            there_core, there_y = c // 4, (y + c % 4) % 4
            base = pl.multiple_of(seat(there_y, 0, there_core) * BOX, QUAD)
            scores = dot_t(qa[pl.ds(base, QUAD), :], ka[...])
            top = jnp.max(scores, axis=1, keepdims=True)
            weights = jnp.exp2((scores - top) * SCALE).astype(BF16)
            summed = dot(weights, va[...])
            ret_out[h, pl.ds(base, QUAD), :] = (summed[:, :HD] / summed[:, HD:]).astype(BF16)
            mine = pl.ds(pl.multiple_of(me * BOX, BOX), BOX)
            for j in range(4):
                there_x = (x + j) % 4
                rows = pl.ds(pl.multiple_of(base + there_x * BOX, BOX), BOX)

                def send(rows=rows, there_x=there_x):
                    pltpu.make_async_remote_copy(
                        src_ref=ret_out.at[h, rows],
                        dst_ref=ret_in.at[h, mine],
                        send_sem=ret_send.at[h],
                        recv_sem=ret_recv.at[h],
                        device_id=(device(there_y, there_x, there_core), plane),
                        device_id_type=MESH,
                    ).start()

                if j == 0:
                    self_here = (c % 4 == 0) & (there_core == core)
                    pl.when(jnp.logical_not(self_here))(send)

                    def keep(rows=rows):
                        ret_in[h, mine, :] = ret_out[h, rows, :]

                    pl.when(self_here)(keep)
                else:
                    send()
            return 0

        lax.fori_loop(0, 8, chunk, 0)

    att_copies = {}

    def restore(h):
        wait_bytes(ret_in.at[h, pl.ds(0, others)], ret_recv.at[h])

        def tokens(c, _):
            base = pl.multiple_of(c * QUAD, QUAD)
            pos = pos_all[h, pl.ds(base, QUAD), :].astype(jnp.int32)
            lane = iota((QUAD, 128), 1)
            pick = jnp.concatenate(
                [(pos == lane + b * 128).astype(BF16) for b in range(ROWS // 128)], axis=1
            )
            att[h, plane, pl.ds(base, QUAD), :] = dot(pick, ret_in[h]).astype(BF16)
            return 0

        lax.fori_loop(0, TOK // QUAD, tokens, 0)
        for step in range(1, PLANES):
            copy = pltpu.make_async_remote_copy(
                src_ref=att.at[h, plane],
                dst_ref=att.at[h, plane],
                send_sem=att_send.at[h, step - 1],
                recv_sem=att_recv.at[h, step - 1],
                device_id=(me, (plane + step) % PLANES),
                device_id_type=MESH,
            )
            copy.start()
            att_copies[h, step] = copy

    attend(0)
    attend(1)
    restore(0)
    attend(2)
    restore(1)
    own_w.wait()
    for copy in w_copies:
        copy.wait()
    for h in range(2):
        for step in range(1, PLANES):
            att_copies[h, step].wait_recv()

    def project_two(c, _):
        rows = pl.ds(pl.multiple_of(c * QUAD, QUAD), QUAD)
        total = jnp.zeros((QUAD, OUT), F32)
        for p in range(PLANES):
            pair = jnp.concatenate([att[0, p, rows, :], att[1, p, rows, :]], axis=1)
            total = total + dot(pair, wcol[p, 0 : 2 * HD, :])
        acc[rows, :] = total
        return 0

    lax.fori_loop(0, TOK // QUAD, project_two, 0)
    restore(2)
    for step in range(1, PLANES):
        att_copies[2, step].wait_recv()

    def project_last(c, _):
        rows = pl.ds(pl.multiple_of(c * QUAD, QUAD), QUAD)
        total = acc[rows, :]
        for p in range(0, PLANES, 2):
            pair = jnp.concatenate([att[2, p, rows, :], att[2, p + 1, rows, :]], axis=1)
            both = jnp.concatenate([wcol[p, 2 * HD :, :], wcol[p + 1, 2 * HD :, :]], axis=0)
            total = total + dot(pair, both)
        out_ref[rows, :] = total.astype(BF16)
        return 0

    lax.fori_loop(0, TOK // QUAD, project_last, 0)

    for h in range(HEADS):
        wait_bytes(outbox.at[h, pl.ds(0, others)], box_send.at[h])
        wait_bytes(ret_out.at[h, pl.ds(0, others)], ret_send.at[h])
        for step in range(1, PLANES):
            att_copies[h, step].wait_send()
    wait_bytes(msg_in.at[pl.ds(0, PEERS - 1)], msg_send)


def shards(queries, keys, values, clusters, cluster_slot, pair_shift, w_out):
    vmem = pl.BlockSpec(memory_space=pltpu.VMEM)
    dma = pltpu.SemaphoreType.DMA
    return pl.pallas_call(
        kernel,
        out_shape=jax.ShapeDtypeStruct((TOK, OUT), BF16),
        in_specs=[vmem] * 6 + [pl.BlockSpec(memory_space=pl.ANY)],
        out_specs=vmem,
        scratch_shapes=[
            pltpu.VMEM((HEADS, ROWS, 3 * HD), BF16),
            pltpu.VMEM((HEADS, ROWS, 3 * HD), BF16),
            pltpu.VMEM((8, SLOTS), F32),
            pltpu.VMEM((PEERS, 8, SLOTS), F32),
            pltpu.VMEM((HEADS, ROWS, HD), BF16),
            pltpu.VMEM((HEADS, ROWS, HD), BF16),
            pltpu.VMEM((HEADS, PLANES, TOK, HD), BF16),
            pltpu.VMEM((PLANES, HEADS * HD, OUT), BF16),
            pltpu.VMEM((TOK, OUT), F32),
            pltpu.VMEM((8, TOK), F32),
            pltpu.VMEM((HEADS, TOK, 128), F32),
            pltpu.VMEM((ROWS, 2 * HD), BF16),
            pltpu.VMEM((ROWS, 2 * HD), BF16),
            pltpu.VMEM((ROWS, 2 * HD), BF16),
            pltpu.VMEM((HEADS, SLOTS, SLOTS), BF16),
            dma((HEADS,)),
            dma((HEADS,)),
            dma,
            dma,
            dma((HEADS,)),
            dma((HEADS,)),
            dma((HEADS, PLANES - 1)),
            dma((HEADS, PLANES - 1)),
            dma((PLANES - 1,)),
            dma((PLANES - 1,)),
            dma,
        ],
        compiler_params=pltpu.CompilerParams(
            collective_id=0, has_side_effects=True, vmem_limit_bytes=62 * 2**20
        ),
        cost_estimate=pl.CostEstimate(
            flops=40 * 10**9, bytes_accessed=10 * 10**6, transcendentals=28 * 10**6
        ),
    )(queries, keys, values, clusters, cluster_slot, pair_shift, w_out)


def solution(mesh):
    in_specs = (
        P("tok", "head"),
        P("tok", "head"),
        P("tok", "head"),
        P("head", "tok"),
        P("head", None),
        P("head", None),
        P("head", None),
    )
    return jax.shard_map(
        shards, mesh=mesh, in_specs=in_specs, out_specs=P("tok", "head"), check_vma=False
    )
```

time: 656 us -> 182 us (0.28); the launches traced: 645 us -> 182 us
  waiting for transfers between devices: 259 us -> 0 us
  Pallas kernels: 0 us -> 179 us
  local copies, waits for them, and re-layouts: 163 us -> 3.22 us
  other arithmetic: 65.2 us -> 0 us
  matrix products: 59.1 us -> 0 us
  loops' own time: 57.6 us -> 0 us
  starting transfers between devices: 28.1 us -> 0 us
  between operations: 13.9 us -> 0.01 us
    pallas_call x0 -> x1, Pallas kernels: none -> 179 us  [shards(): pl.pallas_call(kernel, out_shape=jax.ShapeDtypeStruct((TOK, OUT), BF16),...]
    all_to_all x3 -> x0, waiting for transfers between devices: 169 us -> none  [the longest x1 126 us: shards(): lax.all_to_all(outbox, 'tok', split_axis=1, concat_axis=3, tiled=True)]
    reduce_scatter x1 -> x0, waiting for transfers between devices: 89.6 us -> none  [shards(): lax.psum_scatter(partial_sum.astype(jnp.bfloat16), 'head', scatter_dimens...]
    dot_general x25 -> x0, matrix products: 59.1 us -> none  [the longest x12 29.4 us: normalized(): summed = jnp.dot(weights, value_rows, preferred_element_type=jnp.float32)]
    another operation x1 -> x0, loops' own time: 57.6 us -> none  [attend_slots(): lax.map(per_item, jnp.arange(head_count * groups, dtype=jnp.int32))]
    another operation x11 -> x0, local copies, waits for them, and re-layouts: 38.6 us -> none  [the longest x4 23.4 us: shards(): jnp.stack(filled_list)]
    scatter x3 -> x0, local copies, waits for them, and re-layouts: 33.5 us -> none  [shards(): marked_list.append(jnp.zeros((box_rows,), jnp.bfloat16).at[position[head_...]
    scatter x3 -> x0, other arithmetic: 30.4 us -> none  [shards(): jnp.zeros((box_rows, 3 * HD), jnp.bfloat16).at[position[head_index]]]
  transfers between devices with their start and end apart: 4 -> 0, of which waited for: 3 -> 0; matrix products, arithmetic and copies ran while one was open for 10% -> 0% of each run, Pallas kernels for 0% -> 0%
where the time goes in v1:
time: 182 us
  Pallas kernels  179 us (98%)
  local copies, waits for them, and re-layouts  3.22 us (2%)
    pallas_call x1, Pallas kernels, shards(): pl.pallas_call(kernel, out_shape=jax.ShapeDtypeStruct((TOK, OUT), BF16),...  179 us

profile of v1, /device:TPU:1, one launch (start us, length us, event | category | flops | bytes accessed | tf_op | source)
XLA Modules:
  0.0 181.9 jit_solution(2918798236821473953)
XLA Ops:
  0.0 178.7 %shard_map.73 = bf16[1536,768]{1,0:T(8,128)(2,1)} custom-call(bf16[1536,384]{1,0:T(8,128)(2,1)} %q_ref.1, bf16[1536,384]{1,0:T(8,128)(2,1)} %k_ref.1, bf16[1536,384]{1,0:T(8,128)(2,1)} %v_ref.1, s32[3,1536]{1,0:T(4,128)} %cl_ref.1, s32[3,128]{1,0:T(4,128)} %slot_ref.1, s32[3,128]{1,0:T(4,128)} %shift_ref.1, bf16[384,3072]{1,0:T(8,128)(2,1)} %w_ref.1), custom_call_target="tpu_custom_call" | custom-call | flops 40000000000 | bytes 10000000 | tf_op jit(solution)/shard_map/pallas_call | solution.py:321
  178.7 3.2 %copy.9 = bf16[1536,768]{1,0:T(8,128)(2,1)} copy(bf16[1536,768]{1,0:T(8,128)(2,1)} %shard_map.73) | data formatting | bytes 4718592

commit v2 on v1

--- a/solution.py
+++ b/solution.py
@@ -130,6 +130,41 @@
     def peer_of(g, j):
         return device((y + 2 * g + j // 4 + j) % 4, (x + j) % 4, (core + g // 2) % 2)
 
+    def send_boxes(h, g):
+        for j in range(8):
+            def send(j=j):
+                peer = (peer_of(g, j), plane)
+                k = g * 8 + j
+                pltpu.make_async_remote_copy(
+                    src_ref=outbox.at[h, pl.ds(pl.multiple_of(k * BOX, BOX), BOX)],
+                    dst_ref=inbox.at[h, pl.ds(pl.multiple_of(my_seat * BOX, BOX), BOX)],
+                    send_sem=box_send.at[h],
+                    recv_sem=box_recv.at[h],
+                    device_id=peer,
+                    device_id_type=MESH,
+                ).start()
+                if h == 0:
+                    pltpu.make_async_remote_copy(
+                        src_ref=msg_out,
+                        dst_ref=msg_in.at[my_seat],
+                        send_sem=msg_send,
+                        recv_sem=msg_recv,
+                        device_id=peer,
+                        device_id_type=MESH,
+                    ).start()
+
+            if j == 0:
+                pl.when(g != 0)(send)
+            else:
+                send()
+
+    def send_late(low, high):
+        def group(g, _):
+            send_boxes(HEADS - 1, g)
+            return 0
+
+        lax.fori_loop(low, high, group, 0)
+
     for h in range(HEADS):
         cols = slice(h * HD, (h + 1) * HD)
 
@@ -142,31 +177,8 @@
             rows = jnp.concatenate([q_ref[:, cols], k_ref[:, cols], v_ref[:, cols]], axis=1)
             base = pl.multiple_of(g * 8 * BOX, 8 * BOX)
             outbox[h, pl.ds(base, 8 * BOX), :] = dot(pick, rows).astype(BF16)
-            for j in range(8):
-                def send(g=g, j=j):
-                    peer = (peer_of(g, j), plane)
-                    k = g * 8 + j
-                    pltpu.make_async_remote_copy(
-                        src_ref=outbox.at[h, pl.ds(pl.multiple_of(k * BOX, BOX), BOX)],
-                        dst_ref=inbox.at[h, pl.ds(pl.multiple_of(my_seat * BOX, BOX), BOX)],
-                        send_sem=box_send.at[h],
-                        recv_sem=box_recv.at[h],
-                        device_id=peer,
-                        device_id_type=MESH,
-                    ).start()
-                    if h == 0:
-                        pltpu.make_async_remote_copy(
-                            src_ref=msg_out,
-                            dst_ref=msg_in.at[my_seat],
-                            send_sem=msg_send,
-                            recv_sem=msg_recv,
-                            device_id=peer,
-                            device_id_type=MESH,
-                        ).start()
-                if j == 0:
-                    pl.when(g != 0)(send)
-                else:
-                    send()
+            if h < 2:
+                send_boxes(h, g)
             return 0
 
         lax.fori_loop(0, 4, pack, 0)
@@ -179,7 +191,7 @@
 
     others = (PEERS - 1) * BOX
 
-    def attend(h):
+    def arrive(h):
         wait_bytes(inbox.at[h, pl.ds(0, others)], box_recv.at[h])
         if h == 0:
             wait_bytes(msg_in.at[pl.ds(0, PEERS - 1)], msg_recv)
@@ -204,20 +216,23 @@
 
         lax.fori_loop(0, PEERS // 4, prepare, 0)
 
-        def chunk(c, _):
-            there_core, there_y = c // 4, (y + c % 4) % 4
-            base = pl.multiple_of(seat(there_y, 0, there_core) * BOX, QUAD)
-            scores = dot_t(qa[pl.ds(base, QUAD), :], ka[...])
-            top = jnp.max(scores, axis=1, keepdims=True)
-            weights = jnp.exp2((scores - top) * SCALE).astype(BF16)
-            summed = dot(weights, va[...])
-            ret_out[h, pl.ds(base, QUAD), :] = (summed[:, :HD] / summed[:, HD:]).astype(BF16)
+    def attend(h, low, high):
+        def part(c, _):
+            there_core, half = c // 2, (y // 2 + c % 2) % 2
+            base = pl.multiple_of(seat(half * 2, 0, there_core) * BOX, 2 * QUAD)
+            spans = [pl.ds(pl.multiple_of(base + i * QUAD, QUAD), QUAD) for i in range(2)]
+            scores = [dot_t(qa[span, :], ka[...]) for span in spans]
+            for i in range(2):
+                top = jnp.max(scores[i], axis=1, keepdims=True)
+                weights = jnp.exp2((scores[i] - top) * SCALE).astype(BF16)
+                summed = dot(weights, va[...])
+                ret_out[h, spans[i], :] = (summed[:, :HD] / summed[:, HD:]).astype(BF16)
             mine = pl.ds(pl.multiple_of(me * BOX, BOX), BOX)
-            for j in range(4):
-                there_x = (x + j) % 4
-                rows = pl.ds(pl.multiple_of(base + there_x * BOX, BOX), BOX)
-
-                def send(rows=rows, there_x=there_x):
+            for j in range(8):
+                there_y, there_x = half * 2 + (y + j) % 2, (x + j // 2) % 4
+                rows = pl.ds(pl.multiple_of(seat(there_y, there_x, there_core) * BOX, BOX), BOX)
+
+                def send(rows=rows, there_y=there_y, there_x=there_x):
                     pltpu.make_async_remote_copy(
                         src_ref=ret_out.at[h, rows],
                         dst_ref=ret_in.at[h, mine],
@@ -228,7 +243,7 @@
                     ).start()
 
                 if j == 0:
-                    self_here = (c % 4 == 0) & (there_core == core)
+                    self_here = (c % 2 == 0) & (there_core == core)
                     pl.when(jnp.logical_not(self_here))(send)
 
                     def keep(rows=rows):
@@ -239,9 +254,18 @@
                     send()
             return 0
 
-        lax.fori_loop(0, 8, chunk, 0)
-
-    att_copies = {}
+        lax.fori_loop(low, high, part, 0)
+
+    def gather_copy(h, step, c):
+        rows = pl.ds(pl.multiple_of(c * QUAD, QUAD), QUAD)
+        return pltpu.make_async_remote_copy(
+            src_ref=att.at[h, plane, rows],
+            dst_ref=att.at[h, plane, rows],
+            send_sem=att_send.at[h, step - 1, c],
+            recv_sem=att_recv.at[h, step - 1, c],
+            device_id=(me, (plane + step) % PLANES),
+            device_id_type=MESH,
+        )
 
     def restore(h):
         wait_bytes(ret_in.at[h, pl.ds(0, others)], ret_recv.at[h])
@@ -254,35 +278,37 @@
                 [(pos == lane + b * 128).astype(BF16) for b in range(ROWS // 128)], axis=1
             )
             att[h, plane, pl.ds(base, QUAD), :] = dot(pick, ret_in[h]).astype(BF16)
+            for step in (2, 1, 3):
+                gather_copy(h, step, c).start()
             return 0
 
         lax.fori_loop(0, TOK // QUAD, tokens, 0)
+
+    def gathered(h, c):
         for step in range(1, PLANES):
-            copy = pltpu.make_async_remote_copy(
-                src_ref=att.at[h, plane],
-                dst_ref=att.at[h, plane],
-                send_sem=att_send.at[h, step - 1],
-                recv_sem=att_recv.at[h, step - 1],
-                device_id=(me, (plane + step) % PLANES),
-                device_id_type=MESH,
-            )
-            copy.start()
-            att_copies[h, step] = copy
-
-    attend(0)
-    attend(1)
+            gather_copy(h, step, c).wait_recv()
+
+    arrive(0)
+    attend(0, 0, 4)
+    send_late(0, 2)
+    arrive(1)
+    attend(1, 0, 4)
+    send_late(2, 4)
     restore(0)
-    attend(2)
     restore(1)
+    arrive(2)
+    attend(2, 0, 3)
+    pl.when(core == 0)(lambda: restore(2))
+    attend(2, 3, 4)
+    pl.when(core == 1)(lambda: restore(2))
     own_w.wait()
     for copy in w_copies:
         copy.wait()
-    for h in range(2):
-        for step in range(1, PLANES):
-            att_copies[h, step].wait_recv()
 
     def project_two(c, _):
         rows = pl.ds(pl.multiple_of(c * QUAD, QUAD), QUAD)
+        gathered(0, c)
+        gathered(1, c)
         total = jnp.zeros((QUAD, OUT), F32)
         for p in range(PLANES):
             pair = jnp.concatenate([att[0, p, rows, :], att[1, p, rows, :]], axis=1)
@@ -291,12 +317,10 @@
         return 0
 
     lax.fori_loop(0, TOK // QUAD, project_two, 0)
-    restore(2)
-    for step in range(1, PLANES):
-        att_copies[2, step].wait_recv()
 
     def project_last(c, _):
         rows = pl.ds(pl.multiple_of(c * QUAD, QUAD), QUAD)
+        gathered(2, c)
         total = acc[rows, :]
         for p in range(0, PLANES, 2):
             pair = jnp.concatenate([att[2, p, rows, :], att[2, p + 1, rows, :]], axis=1)
@@ -311,7 +335,8 @@
         wait_bytes(outbox.at[h, pl.ds(0, others)], box_send.at[h])
         wait_bytes(ret_out.at[h, pl.ds(0, others)], ret_send.at[h])
         for step in range(1, PLANES):
-            att_copies[h, step].wait_send()
+            for c in range(TOK // QUAD):
+                gather_copy(h, step, c).wait_send()
     wait_bytes(msg_in.at[pl.ds(0, PEERS - 1)], msg_send)
 
 
@@ -345,8 +370,8 @@
             dma,
             dma((HEADS,)),
             dma((HEADS,)),
-            dma((HEADS, PLANES - 1)),
-            dma((HEADS, PLANES - 1)),
+            dma((HEADS, PLANES - 1, TOK // QUAD)),
+            dma((HEADS, PLANES - 1, TOK // QUAD)),
             dma((PLANES - 1,)),
             dma((PLANES - 1,)),
             dma,

time: 182 us -> 156 us (0.86)
  Pallas kernels: 179 us -> 153 us
    pallas_call x1, Pallas kernels: 179 us -> 153 us  [shards(): pl.pallas_call(kernel, out_shape=jax.ShapeDtypeStruct((TOK, OUT), BF16),...]
where the time goes in v2:
time: 156 us
  Pallas kernels  153 us (98%)
  local copies, waits for them, and re-layouts  3.22 us (2%)
    pallas_call x1, Pallas kernels, shards(): pl.pallas_call(kernel, out_shape=jax.ShapeDtypeStruct((TOK, OUT), BF16),...  153 us
    unnamed x1, local copies, waits for them, and re-layouts  3.22 us

profile of v2, /device:TPU:1, one launch (start us, length us, event | category | flops | bytes accessed | tf_op | source)
XLA Modules:
  0.0 156.3 jit_solution(4296483498593105801)
XLA Ops:
  0.0 153.1 %shard_map.73 = bf16[1536,768]{1,0:T(8,128)(2,1)} custom-call(bf16[1536,384]{1,0:T(8,128)(2,1)} %q_ref.1, bf16[1536,384]{1,0:T(8,128)(2,1)} %k_ref.1, bf16[1536,384]{1,0:T(8,128)(2,1)} %v_ref.1, s32[3,1536]{1,0:T(4,128)} %cl_ref.1, s32[3,128]{1,0:T(4,128)} %slot_ref.1, s32[3,128]{1,0:T(4,128)} %shift_ref.1, bf16[384,3072]{1,0:T(8,128)(2,1)} %w_ref.1), custom_call_target="tpu_custom_call" | custom-call | flops 40000000000 | bytes 10000000 | tf_op jit(solution)/shard_map/pallas_call | solution.py:346
  153.1 3.2 %copy.9 = bf16[1536,768]{1,0:T(8,128)(2,1)} copy(bf16[1536,768]{1,0:T(8,128)(2,1)} %shard_map.73) | data formatting | bytes 4718592

commit v3 on v2

--- a/solution.py
+++ b/solution.py
@@ -21,6 +21,7 @@
 BIG = 1e30
 SCALE = math.log2(math.e) / math.sqrt(HD)
 MESH = pl.DeviceIdType.MESH
+DIRECT = (1,)
 F32 = jnp.float32
 BF16 = jnp.bfloat16
 
@@ -40,11 +41,11 @@
 
 
 def kernel(
-    q_ref, k_ref, v_ref, cl_ref, slot_ref, shift_ref, w_ref, out_ref,
-    outbox, inbox, msg_out, msg_in, ret_out, ret_in, att, wcol, acc,
+    q_hbm, k_hbm, v_hbm, cl_ref, slot_ref, shift_ref, w_ref, out_ref,
+    q_ref, k_ref, v_ref, outbox, inbox, counts, ret_out, ret_in, att, wcol, acc,
     pos_row, pos_all, qa, ka, va, allow,
-    box_send, box_recv, msg_send, msg_recv, ret_send, ret_recv,
-    att_send, att_recv, w_send, w_recv, w_own,
+    box_send, box_recv, count_send, count_recv, ret_send, ret_recv,
+    att_send, att_recv, w_send, w_recv, w_own, load,
 ):
     me = lax.axis_index("tok")
     plane = lax.axis_index("head")
@@ -58,6 +59,11 @@
         return there_core * 16 + there_y * 4 + there_x
 
     my_seat = seat(y, x, core)
+
+    loads = []
+    for i, (source, target) in enumerate(((q_hbm, q_ref), (k_hbm, k_ref), (v_hbm, v_ref))):
+        loads.append(pltpu.make_async_copy(source, target, load.at[i]))
+        loads[i].start()
 
     barrier = pltpu.get_barrier_semaphore()
     for step in range(1, PEERS):
@@ -76,7 +82,8 @@
     before = (same & (col_id < row_id)).astype(BF16)
     after = (same & (row_id < col_id)).astype(BF16)
     box_base = (row_id // CL_DEV * BOX - 1).astype(F32)
-    for h in range(HEADS):
+
+    def place(h):
         slot_line = slot_ref[h : h + 1, :]
         of_cluster = (iota((SLOTS, TOK), 0) == cl_ref[h : h + 1, :]).astype(BF16)
         slot_rows = jnp.broadcast_to(slot_line.astype(F32), (8, SLOTS)).astype(BF16)
@@ -97,18 +104,118 @@
             pos_all[h, lanes, :] = jnp.broadcast_to(line, (128, 128)).T
         count_line = dot_t(jnp.ones((8, TOK), BF16), hot_b)
         low = dot(count_line.astype(BF16), after)
-        msg_out[2 * h : 2 * h + 1, :] = low[0:1]
-        msg_out[2 * h + 1 : 2 * h + 2, :] = (low + count_line)[0:1]
+        counts[me, 2 * h : 2 * h + 1, :] = low[0:1]
+        counts[me, 2 * h + 1 : 2 * h + 2, :] = (low + count_line)[0:1]
         placed = (row_id == slot_line).astype(BF16)
         shift_rows = jnp.broadcast_to(shift_ref[h : h + 1, :].astype(F32), (8, SLOTS))
         shift = dot_t(shift_rows.astype(BF16), placed)[0:1].astype(jnp.int32)
         mate = col_id // CL_DEV * CL_DEV + (col_id % CL_DEV + shift) % CL_DEV
         allow[h] = ((row_id == col_id) | (row_id == mate)).astype(BF16)
-    msg_out[6:8, :] = jnp.zeros((2, 128), F32)
-    msg_in[my_seat] = msg_out[...]
-
+    def peer_of(g, j):
+        return device((y + 2 * g + j // 4 + j) % 4, (x + j) % 4, (core + g // 2) % 2)
+
+    def send_boxes(h, g):
+        for j in range(8):
+            def send(j=j):
+                peer = (peer_of(g, j), plane)
+                k = g * 8 + j
+                pltpu.make_async_remote_copy(
+                    src_ref=outbox.at[h, pl.ds(pl.multiple_of(k * BOX, BOX), BOX)],
+                    dst_ref=inbox.at[h, pl.ds(pl.multiple_of(my_seat * BOX, BOX), BOX)],
+                    send_sem=box_send.at[h],
+                    recv_sem=box_recv.at[h],
+                    device_id=peer,
+                    device_id_type=MESH,
+                ).start()
+
+            if j == 0:
+                pl.when(g != 0)(send)
+            else:
+                send()
+
+    def send_late(low, high):
+        def group(g, _):
+            send_boxes(HEADS - 1, g)
+            return 0
+
+        lax.fori_loop(low, high, group, 0)
+
+    def wait_bytes(ref, semaphore):
+        pltpu.make_async_copy(ref, ref, semaphore).wait()
+
+    others = (PEERS - 1) * BOX
+
+    def count_copy(i):
+        first, number, there = (
+            (me, 1, device(y, x, 1 - core))
+            if i == 0
+            else (2 * chip, 2, device(y, (x + i) % 4, core))
+            if i < 4
+            else (8 * y, 8, device((y + i - 3) % 4, x, core))
+        )
+        return pltpu.make_async_remote_copy(
+            src_ref=counts.at[pl.ds(first, number)],
+            dst_ref=counts.at[pl.ds(first, number)],
+            send_sem=count_send.at[i],
+            recv_sem=count_recv.at[i],
+            device_id=(there, plane),
+            device_id_type=MESH,
+        )
+
+    def count_came(i):
+        first, number = (
+            (2 * chip + 1 - core, 1)
+            if i == 0
+            else (2 * (4 * y + (x + 4 - i) % 4), 2)
+            if i < 4
+            else (8 * ((y + 7 - i) % 4), 8)
+        )
+        wait_bytes(counts.at[pl.ds(first, number)], count_recv.at[i])
+
+    def spread_counts(g):
+        def along_x():
+            count_came(0)
+            for i in range(1, 4):
+                count_copy(i).start()
+
+        def along_y():
+            for i in range(1, 4):
+                count_came(i)
+            for i in range(4, 7):
+                count_copy(i).start()
+
+        pl.when(g == 1)(along_x)
+        pl.when(g == 3)(along_y)
+
+    def fill(h):
+        cols = slice(h * HD, (h + 1) * HD)
+
+        def pack(g, _):
+            if h == 0:
+                spread_counts(g)
+            pos = pos_row[h : h + 1, :].astype(jnp.int32)
+            picks = []
+            for j in range(8):
+                picks.append((iota((BOX, TOK), 0) + peer_of(g, j) * BOX == pos).astype(BF16))
+            pick = jnp.concatenate(picks, axis=0)
+            rows = jnp.concatenate([q_ref[:, cols], k_ref[:, cols], v_ref[:, cols]], axis=1)
+            base = pl.multiple_of(g * 8 * BOX, 8 * BOX)
+            outbox[h, pl.ds(base, 8 * BOX), :] = dot(pick, rows).astype(BF16)
+            if h < 2:
+                send_boxes(h, g)
+            return 0
+
+        lax.fori_loop(0, 4, pack, 0)
+        inbox[h, pl.ds(pl.multiple_of(my_seat * BOX, BOX), BOX), :] = outbox[h, 0:BOX, :]
+
+    for h in range(HEADS):
+        place(h)
+    counts[me, 6:8, :] = jnp.zeros((2, SLOTS), F32)
+    for copy in loads:
+        copy.wait()
     pl.semaphore_wait(barrier, PEERS - 1 + PLANES - 1)
-
+    count_copy(0).start()
+    fill(0)
     own_w = pltpu.make_async_copy(
         w_ref.at[:, pl.ds(pl.multiple_of(plane * OUT, 128), OUT)], wcol.at[plane], w_own
     )
@@ -127,74 +234,13 @@
         copy.start()
         w_copies.append(copy)
 
-    def peer_of(g, j):
-        return device((y + 2 * g + j // 4 + j) % 4, (x + j) % 4, (core + g // 2) % 2)
-
-    def send_boxes(h, g):
-        for j in range(8):
-            def send(j=j):
-                peer = (peer_of(g, j), plane)
-                k = g * 8 + j
-                pltpu.make_async_remote_copy(
-                    src_ref=outbox.at[h, pl.ds(pl.multiple_of(k * BOX, BOX), BOX)],
-                    dst_ref=inbox.at[h, pl.ds(pl.multiple_of(my_seat * BOX, BOX), BOX)],
-                    send_sem=box_send.at[h],
-                    recv_sem=box_recv.at[h],
-                    device_id=peer,
-                    device_id_type=MESH,
-                ).start()
-                if h == 0:
-                    pltpu.make_async_remote_copy(
-                        src_ref=msg_out,
-                        dst_ref=msg_in.at[my_seat],
-                        send_sem=msg_send,
-                        recv_sem=msg_recv,
-                        device_id=peer,
-                        device_id_type=MESH,
-                    ).start()
-
-            if j == 0:
-                pl.when(g != 0)(send)
-            else:
-                send()
-
-    def send_late(low, high):
-        def group(g, _):
-            send_boxes(HEADS - 1, g)
-            return 0
-
-        lax.fori_loop(low, high, group, 0)
-
-    for h in range(HEADS):
-        cols = slice(h * HD, (h + 1) * HD)
-
-        def pack(g, _, h=h, cols=cols):
-            pos = pos_row[h : h + 1, :].astype(jnp.int32)
-            picks = []
-            for j in range(8):
-                picks.append((iota((BOX, TOK), 0) + peer_of(g, j) * BOX == pos).astype(BF16))
-            pick = jnp.concatenate(picks, axis=0)
-            rows = jnp.concatenate([q_ref[:, cols], k_ref[:, cols], v_ref[:, cols]], axis=1)
-            base = pl.multiple_of(g * 8 * BOX, 8 * BOX)
-            outbox[h, pl.ds(base, 8 * BOX), :] = dot(pick, rows).astype(BF16)
-            if h < 2:
-                send_boxes(h, g)
-            return 0
-
-        lax.fori_loop(0, 4, pack, 0)
-        inbox[h, pl.ds(pl.multiple_of(my_seat * BOX, BOX), BOX), :] = outbox[h, 0:BOX, :]
+    fill(1)
+    fill(2)
 
     va[:, HD:] = jnp.ones((ROWS, HD), BF16)
-
-    def wait_bytes(ref, semaphore):
-        pltpu.make_async_copy(ref, ref, semaphore).wait()
-
-    others = (PEERS - 1) * BOX
 
     def arrive(h):
         wait_bytes(inbox.at[h, pl.ds(0, others)], box_recv.at[h])
-        if h == 0:
-            wait_bytes(msg_in.at[pl.ds(0, PEERS - 1)], msg_recv)
 
         def prepare(s, _):
             base = pl.multiple_of(s * QUAD, QUAD)
@@ -202,8 +248,9 @@
             mine = iota((BOX, SLOTS), 1) // CL_DEV == me
             tags = []
             for j in range(4):
-                low = msg_in[s * 4 + j, 2 * h : 2 * h + 1, :]
-                high = msg_in[s * 4 + j, 2 * h + 1 : 2 * h + 2, :]
+                sender = device(s % 4, j, s // 4)
+                low = counts[sender, 2 * h : 2 * h + 1, :]
+                high = counts[sender, 2 * h + 1 : 2 * h + 2, :]
                 tags.append(((at >= low) & (at < high) & mine).astype(BF16))
             tag = jnp.concatenate(tags, axis=0)
             box = inbox[h, pl.ds(base, QUAD), :]
@@ -216,8 +263,10 @@
 
         lax.fori_loop(0, PEERS // 4, prepare, 0)
 
-    def attend(h, low, high):
+    def attend(h, hooks):
         def part(c, _):
+            for at, when, hook in hooks:
+                pl.when((c == at) & when)(hook)
             there_core, half = c // 2, (y // 2 + c % 2) % 2
             base = pl.multiple_of(seat(half * 2, 0, there_core) * BOX, 2 * QUAD)
             spans = [pl.ds(pl.multiple_of(base + i * QUAD, QUAD), QUAD) for i in range(2)]
@@ -254,18 +303,42 @@
                     send()
             return 0
 
-        lax.fori_loop(low, high, part, 0)
-
-    def gather_copy(h, step, c):
-        rows = pl.ds(pl.multiple_of(c * QUAD, QUAD), QUAD)
+        lax.fori_loop(0, 4, part, 0)
+
+    left, right = (plane + PLANES - 1) % PLANES, (plane + 1) % PLANES
+    half = QUAD // 2
+
+    def gather_copy(h, way, c):
+        first = c * QUAD + (half if way == 3 else 0)
+        rows = pl.ds(pl.multiple_of(first, half), half if way >= 2 else QUAD)
+        onward = way >= 2 and h not in DIRECT
+        owner = (left, right)[way % 2] if onward else plane
+        there = (plane + 2) % PLANES if way >= 2 and not onward else (right, left)[way % 2]
         return pltpu.make_async_remote_copy(
-            src_ref=att.at[h, plane, rows],
-            dst_ref=att.at[h, plane, rows],
-            send_sem=att_send.at[h, step - 1, c],
-            recv_sem=att_recv.at[h, step - 1, c],
-            device_id=(me, (plane + step) % PLANES),
+            src_ref=att.at[h, owner, rows],
+            dst_ref=att.at[h, owner, rows],
+            send_sem=att_send.at[h, way, c],
+            recv_sem=att_recv.at[h, way, c],
+            device_id=(me, there),
             device_id_type=MESH,
         )
+
+    def forward(h, c):
+        if h in DIRECT:
+            return
+        for way in range(2):
+            gather_copy(h, way, c).wait_recv()
+            gather_copy(h, way + 2, c).start()
+
+    def forward_all(h):
+        if h in DIRECT:
+            return
+
+        def one(c, _):
+            forward(h, c)
+            return 0
+
+        lax.fori_loop(0, TOK // QUAD, one, 0)
 
     def restore(h):
         wait_bytes(ret_in.at[h, pl.ds(0, others)], ret_recv.at[h])
@@ -278,32 +351,32 @@
                 [(pos == lane + b * 128).astype(BF16) for b in range(ROWS // 128)], axis=1
             )
             att[h, plane, pl.ds(base, QUAD), :] = dot(pick, ret_in[h]).astype(BF16)
-            for step in (2, 1, 3):
-                gather_copy(h, step, c).start()
+            for way in range(4 if h in DIRECT else 2):
+                gather_copy(h, way, c).start()
             return 0
 
         lax.fori_loop(0, TOK // QUAD, tokens, 0)
 
     def gathered(h, c):
-        for step in range(1, PLANES):
-            gather_copy(h, step, c).wait_recv()
-
+        for way in range(0 if h in DIRECT else 2, 4):
+            gather_copy(h, way, c).wait_recv()
+
+    for i in range(4, 7):
+        count_came(i)
     arrive(0)
-    attend(0, 0, 4)
-    send_late(0, 2)
+    attend(0, [])
+    send_late(0, 1)
     arrive(1)
-    attend(1, 0, 4)
-    send_late(2, 4)
+    attend(1, [])
+    send_late(1, 4)
     restore(0)
-    restore(1)
-    arrive(2)
-    attend(2, 0, 3)
-    pl.when(core == 0)(lambda: restore(2))
-    attend(2, 3, 4)
-    pl.when(core == 1)(lambda: restore(2))
     own_w.wait()
     for copy in w_copies:
         copy.wait()
+    forward_all(0)
+    restore(1)
+    arrive(2)
+    attend(2, [])
 
     def project_two(c, _):
         rows = pl.ds(pl.multiple_of(c * QUAD, QUAD), QUAD)
@@ -316,6 +389,8 @@
         acc[rows, :] = total
         return 0
 
+    restore(2)
+    forward_all(2)
     lax.fori_loop(0, TOK // QUAD, project_two, 0)
 
     def project_last(c, _):
@@ -331,27 +406,31 @@
 
     lax.fori_loop(0, TOK // QUAD, project_last, 0)
 
+    for i in range(7):
+        count_copy(i).wait_send()
     for h in range(HEADS):
         wait_bytes(outbox.at[h, pl.ds(0, others)], box_send.at[h])
         wait_bytes(ret_out.at[h, pl.ds(0, others)], ret_send.at[h])
-        for step in range(1, PLANES):
+        for way in range(4):
             for c in range(TOK // QUAD):
-                gather_copy(h, step, c).wait_send()
-    wait_bytes(msg_in.at[pl.ds(0, PEERS - 1)], msg_send)
+                gather_copy(h, way, c).wait_send()
 
 
 def shards(queries, keys, values, clusters, cluster_slot, pair_shift, w_out):
     vmem = pl.BlockSpec(memory_space=pltpu.VMEM)
+    hbm = pl.BlockSpec(memory_space=pl.ANY)
     dma = pltpu.SemaphoreType.DMA
     return pl.pallas_call(
         kernel,
         out_shape=jax.ShapeDtypeStruct((TOK, OUT), BF16),
-        in_specs=[vmem] * 6 + [pl.BlockSpec(memory_space=pl.ANY)],
+        in_specs=[hbm] * 3 + [vmem] * 3 + [hbm],
         out_specs=vmem,
         scratch_shapes=[
+            pltpu.VMEM((TOK, HEADS * HD), BF16),
+            pltpu.VMEM((TOK, HEADS * HD), BF16),
+            pltpu.VMEM((TOK, HEADS * HD), BF16),
             pltpu.VMEM((HEADS, ROWS, 3 * HD), BF16),
             pltpu.VMEM((HEADS, ROWS, 3 * HD), BF16),
-            pltpu.VMEM((8, SLOTS), F32),
             pltpu.VMEM((PEERS, 8, SLOTS), F32),
             pltpu.VMEM((HEADS, ROWS, HD), BF16),
             pltpu.VMEM((HEADS, ROWS, HD), BF16),
@@ -366,15 +445,16 @@
             pltpu.VMEM((HEADS, SLOTS, SLOTS), BF16),
             dma((HEADS,)),
             dma((HEADS,)),
-            dma,
-            dma,
+            dma((7,)),
+            dma((7,)),
             dma((HEADS,)),
             dma((HEADS,)),
-            dma((HEADS, PLANES - 1, TOK // QUAD)),
-            dma((HEADS, PLANES - 1, TOK // QUAD)),
+            dma((HEADS, 4, TOK // QUAD)),
+            dma((HEADS, 4, TOK // QUAD)),
             dma((PLANES - 1,)),
             dma((PLANES - 1,)),
             dma,
+            dma((3,)),
         ],
         compiler_params=pltpu.CompilerParams(
             collective_id=0, has_side_effects=True, vmem_limit_bytes=62 * 2**20

time: 156 us -> 150 us (0.962)
  Pallas kernels: 153 us -> 146 us
    pallas_call x1, Pallas kernels: 153 us -> 146 us  [shards(): pl.pallas_call(kernel, out_shape=jax.ShapeDtypeStruct((TOK, OUT), BF16),...]
where the time goes in v3:
time: 150 us
  Pallas kernels  146 us (97%)
  local copies, waits for them, and re-layouts  3.22 us (2%)
    pallas_call x1, Pallas kernels, shards(): pl.pallas_call(kernel, out_shape=jax.ShapeDtypeStruct((TOK, OUT), BF16),...  146 us
    unnamed x1, local copies, waits for them, and re-layouts  3.22 us

profile of v3, /device:TPU:1, one launch (start us, length us, event | category | flops | bytes accessed | tf_op | source)
XLA Modules:
  0.0 149.6 jit_solution(13492751615939071576)
XLA Ops:
  0.0 146.4 %shard_map.73 = bf16[1536,768]{1,0:T(8,128)(2,1)} custom-call(bf16[1536,384]{1,0:T(8,128)(2,1)} %q_hbm.1, bf16[1536,384]{1,0:T(8,128)(2,1)} %k_hbm.1, bf16[1536,384]{1,0:T(8,128)(2,1)} %v_hbm.1, s32[3,1536]{1,0:T(4,128)} %cl_ref.1, s32[3,128]{1,0:T(4,128)} %slot_ref.1, s32[3,128]{1,0:T(4,128)} %shift_ref.1, bf16[384,3072]{1,0:T(8,128)(2,1)} %w_ref.1), custom_call_target="tpu_custom_call" | custom-call | flops 40000000000 | bytes 10000000 | tf_op jit(solution)/shard_map/pallas_call | solution.py:423
  146.4 3.2 %copy.9 = bf16[1536,768]{1,0:T(8,128)(2,1)} copy(bf16[1536,768]{1,0:T(8,128)(2,1)} %shard_map.73) | data formatting | bytes 4718592

commit v4 on v3

--- a/solution.py
+++ b/solution.py
@@ -367,8 +367,7 @@
     attend(0, [])
     send_late(0, 1)
     arrive(1)
-    attend(1, [])
-    send_late(1, 4)
+    attend(1, [(3, True, lambda: send_late(1, 4))])
     restore(0)
     own_w.wait()
     for copy in w_copies:

time: 150 us -> 153 us (1.020)
  Pallas kernels: 146 us -> 150 us
    pallas_call x1, Pallas kernels: 146 us -> 150 us  [shards(): pl.pallas_call(kernel, out_shape=jax.ShapeDtypeStruct((TOK, OUT), BF16),...]
where the time goes in v4:
time: 153 us
  Pallas kernels  150 us (98%)
  local copies, waits for them, and re-layouts  3.22 us (2%)
    pallas_call x1, Pallas kernels, shards(): pl.pallas_call(kernel, out_shape=jax.ShapeDtypeStruct((TOK, OUT), BF16),...  150 us
    unnamed x1, local copies, waits for them, and re-layouts  3.22 us

profile of v4, /device:TPU:1, one launch (start us, length us, event | category | flops | bytes accessed | tf_op | source)
XLA Modules:
  0.0 153.2 jit_solution(2522022858765603567)
XLA Ops:
  0.0 150.0 %shard_map.73 = bf16[1536,768]{1,0:T(8,128)(2,1)} custom-call(bf16[1536,384]{1,0:T(8,128)(2,1)} %q_hbm.1, bf16[1536,384]{1,0:T(8,128)(2,1)} %k_hbm.1, bf16[1536,384]{1,0:T(8,128)(2,1)} %v_hbm.1, s32[3,1536]{1,0:T(4,128)} %cl_ref.1, s32[3,128]{1,0:T(4,128)} %slot_ref.1, s32[3,128]{1,0:T(4,128)} %shift_ref.1, bf16[384,3072]{1,0:T(8,128)(2,1)} %w_ref.1), custom_call_target="tpu_custom_call" | custom-call | flops 40000000000 | bytes 10000000 | tf_op jit(solution)/shard_map/pallas_call | solution.py:422
  150.0 3.2 %copy.9 = bf16[1536,768]{1,0:T(8,128)(2,1)} copy(bf16[1536,768]{1,0:T(8,128)(2,1)} %shard_map.73) | data formatting | bytes 4718592
